TPU v7x, 32 devices: a whole 2x2x4 slice. The times are simulated.
32 devices in a mesh: tm: 8 (over y, x, core), space: 4 (over z).
Axes of the slice: x: 2, y: 2, z: 4, core: 2. Of those that a mesh axis runs over, the one named last changes fastest.
Arguments:
- base: float32 [8, 3, 16, 64, 128], P('tm', None, 'space')
- tangent: float32 [8, 4, 3, 16, 64, 128], P('tm', None, None, 'space')
Outputs:
- correction: float32 [8, 3, 16, 64, 128], P('tm', None, 'space')
- defect: float32 [8, 3, 16, 64, 128], P('tm', None, 'space')
- coefs: float32 [8, 4], P('tm')
All inputs are finite; a program needn't handle non-finite values.
Results may differ from a plain program's by a relative error of at most 0.0003.
Values sent between devices are 32-bit elements; how exact they have to be, the bound alone decides.
A program may use at most 128 MiB of HBM per device.

v0:
```python
import functools

import jax
import jax.numpy as jnp
from jax import lax
from jax.experimental import pallas as pl
from jax.experimental.pallas import tpu as pltpu
from jax.sharding import PartitionSpec as P

MESH = pl.DeviceIdType.MESH
STEPS = 3
COLS = 4
LANES = 128
GRAM = COLS * COLS
ENTRIES = GRAM + COLS * (COLS + 1)
ROWS = 40

time_step = 0.05
viscosity = 0.4
forcing_amp = 1.0
wave_number = 4.0

KEEP = 1.0 - 6.0 * time_step * viscosity
SPREAD = time_step * viscosity
HALF = 0.5 * time_step


def neighbours(ref, lead, plane):
    centre = ref[(*lead, plane)]
    rows, lanes = centre.shape
    east = ref[(*lead, plane + 1)]
    west = ref[(*lead, plane - 1)]
    north = pltpu.roll(centre, rows - 1, 0)
    south = pltpu.roll(centre, 1, 0)
    upper = pltpu.roll(centre, lanes - 1, 1)
    lower = pltpu.roll(centre, 1, 1)
    total = (east + west) + (north + south) + (upper + lower)
    return centre, total, east - west, north - south, upper - lower


def dot_tiles(a, b):
    prod = a * b
    return jnp.sum(prod.reshape(prod.shape[0] // 8, 8, prod.shape[1]), axis=0)


def eliminate(rows, pivoting):
    rows = [list(r) for r in rows]
    n = len(rows)
    for k in range(n):
        if pivoting:
            for r in range(k + 1, n):
                swap = jnp.abs(rows[r][k]) > jnp.abs(rows[k][k])
                for c in range(k, len(rows[k])):
                    high, low = rows[k][c], rows[r][c]
                    rows[k][c] = jnp.where(swap, low, high)
                    rows[r][c] = jnp.where(swap, high, low)
        inverse = 1.0 / rows[k][k]
        for c in range(k + 1, len(rows[k])):
            rows[k][c] = rows[k][c] * inverse
        for r in range(n):
            if r != k:
                factor = rows[r][k]
                for c in range(k + 1, len(rows[k])):
                    rows[r][c] = rows[r][c] - factor * rows[k][c]
    return [r[n:] for r in rows]


def shooting_coefs(entry, n_tm):
    def roll(x, by):
        return pltpu.roll(x, by % LANES, 1)

    gram = [[roll(entry(a * COLS + b), -1) for b in range(COLS)] for a in range(COLS)]
    cross = [[entry(GRAM + k * COLS + j) for k in range(COLS + 1)] for j in range(COLS)]
    maps = eliminate([g + c for g, c in zip(gram, cross)], False)
    maps = [[roll(x, 1) for x in row] for row in maps]
    for level in range(n_tm.bit_length() - 1):
        earlier = [[roll(x, 1 << level) for x in row] for row in maps]
        new = []
        for r in range(COLS):
            row = []
            for c in range(COLS + 1):
                terms = [maps[r][k] * earlier[k][c] for k in range(COLS)]
                value = (terms[0] + terms[1]) + (terms[2] + terms[3])
                row.append(value + maps[r][COLS] if c == COLS else value)
            new.append(row)
        maps = new
    system = [
        [(1.0 if r == c else 0.0) - maps[r][c] for c in range(COLS)] + [maps[r][COLS]]
        for r in range(COLS)
    ]
    return [r[0] for r in eliminate(system, True)]


def kernel(
    n_tm, n_space, base_ref, tangent_ref, corr_ref, defect_ref, coefs_ref,
    flow, grads, tang, work, push, base_next, tang_next, acc, share, table,
    corr, defect,
    local_sem, send_sem, recv_sem, tm_send, tm_recv,
    share_send, share_recv, table_send, table_recv, out_sem,
):
    tm, space = lax.axis_index("tm"), lax.axis_index("space")
    nx = base_ref.shape[2]
    ny, nz = base_ref.shape[3:]
    wide = nx + 2 * STEPS
    up, down = lax.rem(space + 1, n_space), lax.rem(space + n_space - 1, n_space)
    before = lax.rem(tm + n_tm - 1, n_tm)

    barrier = pltpu.get_barrier_semaphore()
    for d in range(1, n_space):
        pl.semaphore_signal(
            barrier, inc=1, device_id={"space": lax.rem(space + d, n_space)}, device_id_type=MESH
        )
    for d in range(1, n_tm):
        pl.semaphore_signal(
            barrier, inc=1, device_id={"tm": lax.rem(tm + d, n_tm)}, device_id_type=MESH
        )
    own = pl.ds(STEPS, nx)
    local = [
        pltpu.make_async_copy(base_ref.at[0], flow.at[0, :, own], local_sem.at[0]),
        pltpu.make_async_copy(tangent_ref.at[0], tang.at[:, :, own], local_sem.at[1]),
    ]
    for copy in local:
        copy.start()
    pl.semaphore_wait(barrier, n_space + n_tm - 2)

    def halo(chunk, side):
        source = pl.ds(nx - STEPS, STEPS) if side == 0 else pl.ds(0, STEPS)
        target = pl.ds(0, STEPS) if side == 0 else pl.ds(nx + STEPS, STEPS)
        if isinstance(chunk, int) and chunk == 0:
            src, dst = base_ref.at[0, :, source], flow.at[0, :, target]
        else:
            src, dst = tangent_ref.at[0, chunk - 1, :, source], tang.at[chunk - 1, :, target]
        return pltpu.make_async_remote_copy(
            src_ref=src, dst_ref=dst,
            send_sem=send_sem.at[chunk, side], recv_sem=recv_sem.at[chunk, side],
            device_id={"space": up if side == 0 else down}, device_id_type=MESH,
        )

    def tm_copy(which):
        src, dst = ((base_ref.at[0], base_next), (tangent_ref.at[0], tang_next))[which]
        return pltpu.make_async_remote_copy(
            src_ref=src, dst_ref=dst, send_sem=tm_send.at[which], recv_sem=tm_recv.at[which],
            device_id={"tm": before}, device_id_type=MESH,
        )

    for chunk in (0, 1):
        for side in (0, 1):
            halo(chunk, side).start()
    for which in (0, 1):
        tm_copy(which).start()

    height = lax.broadcasted_iota(jnp.int32, (ny, nz), 0).astype(jnp.float32)
    drive = (time_step * forcing_amp) * jnp.sin(2.0 * jnp.pi * wave_number * height / ny)

    for copy in local:
        copy.wait()
    acc[...] = jnp.zeros_like(acc)
    pairs = [(a, b) for a in range(COLS) for b in range(a, COLS)]

    def gram_step(i, sums):
        comp, plane = i // nx, i % nx + STEPS
        cols = [tang[k, comp, plane] for k in range(COLS)]
        return tuple(s + dot_tiles(cols[a], cols[b]) for s, (a, b) in zip(sums, pairs))

    zero = jnp.zeros((8, nz), jnp.float32)
    sums = lax.fori_loop(0, 3 * nx, gram_step, (zero,) * len(pairs))
    for s, (a, b) in zip(sums, pairs):
        acc[a * COLS + b] = s
        if a != b:
            acc[b * COLS + a] = s

    for side in (0, 1):
        halo(0, side).wait()
    for side in (0, 1):
        halo(2, side).start()
    for t in range(STEPS):

        def flow_step(plane, carry):
            speed = [HALF * flow[t, d, plane] for d in range(3)]
            for c in range(3):
                centre, total, *diffs = neighbours(flow, (t, c), plane)
                value = KEEP * centre + SPREAD * total
                value = value - (speed[0] * diffs[0] + speed[1] * diffs[1] + speed[2] * diffs[2])
                if c == 0:
                    value = value + drive
                flow[t + 1, c, plane] = value
                for d in range(3):
                    grads[t, 3 * c + d, plane] = HALF * diffs[d]
            return carry

        lax.fori_loop(t + 1, wide - t - 1, flow_step, 0)

    for which in (0, 1):
        tm_copy(which).wait()

    def end_step(i, sums):
        comp, plane = i // nx, i % nx
        gap = flow[STEPS, comp, plane + STEPS] - base_next[comp, plane]
        base_next[comp, plane] = gap
        return tuple(s + dot_tiles(tang_next[j, comp, plane], gap) for j, s in enumerate(sums))

    sums = lax.fori_loop(0, 3 * nx, end_step, (zero,) * COLS)
    for j, s in enumerate(sums):
        acc[GRAM + COLS * COLS + j] = s

    def column(k, carry):
        for side in (0, 1):
            halo(k + 1, side).wait()

        @pl.when(k + 3 < COLS + 1)
        def _():
            for side in (0, 1):
                halo(k + 3, side).start()

        for t in range(STEPS):

            def tangent_step(plane, sums):
                src, lead = (tang, (k,)) if t == 0 else (work, (t - 1,))
                speed = [HALF * flow[t, d, plane] for d in range(3)]
                own_at = [src[(*lead, d, plane)] for d in range(3)]
                for c in range(3):
                    centre, total, *diffs = neighbours(src, (*lead, c), plane)
                    value = KEEP * centre + SPREAD * total
                    value = value - (
                        speed[0] * diffs[0] + speed[1] * diffs[1] + speed[2] * diffs[2]
                    )
                    value = value - (
                        own_at[0] * grads[t, 3 * c, plane]
                        + own_at[1] * grads[t, 3 * c + 1, plane]
                        + own_at[2] * grads[t, 3 * c + 2, plane]
                    )
                    if t < STEPS - 1:
                        work[t, c, plane] = value
                    else:
                        push[k, c, plane - STEPS] = value
                        sums = tuple(
                            s + dot_tiles(tang_next[j, c, plane - STEPS], value)
                            for j, s in enumerate(sums)
                        )
                return sums

            last = t == STEPS - 1
            sums = lax.fori_loop(
                t + 1, wide - t - 1, tangent_step, (zero,) * COLS if last else ()
            )
        for j, s in enumerate(sums):
            acc[GRAM + k * COLS + j] = s
        return carry

    lax.fori_loop(0, COLS, column, 0)

    by_entry = jnp.sum(jnp.sum(acc[...], axis=1), axis=1, keepdims=True)
    row_id = lax.broadcasted_iota(jnp.int32, (ROWS, LANES), 0)
    lane_id = lax.broadcasted_iota(jnp.int32, (ROWS, LANES), 1)
    packed = jnp.sum(jnp.where(row_id == lane_id, by_entry, 0.0), axis=0, keepdims=True)
    share[space] = jnp.broadcast_to(packed, (8, LANES))

    def share_copy(d):
        return pltpu.make_async_remote_copy(
            src_ref=share.at[space], dst_ref=share.at[space],
            send_sem=share_send.at[d], recv_sem=share_recv.at[d],
            device_id={"space": lax.rem(space + d, n_space)}, device_id_type=MESH,
        )

    def table_copy(d):
        return pltpu.make_async_remote_copy(
            src_ref=table.at[tm], dst_ref=table.at[tm],
            send_sem=table_send.at[d], recv_sem=table_recv.at[d],
            device_id={"tm": lax.rem(tm + d, n_tm)}, device_id_type=MESH,
        )

    for d in range(1, n_space):
        share_copy(d).start()
    for d in range(1, n_space):
        share_copy(d).wait()
    table[tm] = functools.reduce(jnp.add, [share[s] for s in range(n_space)])
    for d in range(1, n_tm):
        table_copy(d).start()
    for d in range(1, n_tm):
        table_copy(d).wait()

    sub = lax.broadcasted_iota(jnp.int32, (8, LANES), 0)
    groups = []
    for g in range(max(n_tm // 8, 1)):
        tile = jnp.zeros((8, LANES), jnp.float32)
        for s in range(8):
            tile = jnp.where(sub == s, table[(8 * g + s) % n_tm], tile)
        groups.append(tile)
    square = jnp.concatenate(groups * (LANES // (8 * len(groups))), axis=0)
    flipped = square.T
    coefs = shooting_coefs(lambda e: flipped[e : e + 1], n_tm)

    lane = lax.broadcasted_iota(jnp.int32, (1, LANES), 1)
    mine = lane == tm
    following = lane == lax.rem(tm + 1, n_tm)
    both = jnp.concatenate(
        [jnp.where(mine, x, 0.0) for x in coefs] + [jnp.where(following, x, 0.0) for x in coefs],
        axis=0,
    )
    values = jnp.sum(both, axis=1, keepdims=True)
    own_c = [values[k : k + 1] for k in range(COLS)]
    next_c = [values[COLS + k : COLS + k + 1] for k in range(COLS)]
    places = lax.broadcasted_iota(jnp.int32, (1, COLS), 1)
    out = jnp.zeros((1, COLS), jnp.float32)
    for k in range(COLS):
        out = jnp.where(places == k, own_c[k], out)
    coefs_ref[...] = out

    def out_copy(which, comp):
        src, dst = ((corr, corr_ref), (defect, defect_ref))[which]
        return pltpu.make_async_copy(src.at[comp], dst.at[0, comp], out_sem.at[which, comp])

    own_b = [jnp.broadcast_to(x, (8, LANES)) for x in own_c]
    next_b = [jnp.broadcast_to(x, (8, LANES)) for x in next_c]

    def scaled(coef, array):
        return (array.reshape(ny // 8, 8, nz) * coef[None]).reshape(ny, nz)

    for comp in range(3):

        def finish(plane, carry):
            terms = [scaled(own_b[k], tang[k, comp, plane + STEPS]) for k in range(COLS)]
            corr[comp, plane] = (terms[0] + terms[1]) + (terms[2] + terms[3])
            value = base_next[comp, plane]
            for k in range(COLS):
                value = value + (
                    scaled(own_b[k], push[k, comp, plane])
                    - scaled(next_b[k], tang_next[k, comp, plane])
                )
            defect[comp, plane] = value
            return carry

        lax.fori_loop(0, nx, finish, 0)
        out_copy(0, comp).start()
        out_copy(1, comp).start()
    for comp in range(3):
        out_copy(0, comp).wait()
        out_copy(1, comp).wait()


def body(n_tm, n_space, base, tangent):
    _, comps, nx, ny, nz = base.shape
    wide = nx + 2 * STEPS
    f32 = jnp.float32
    vmem = pltpu.VMEM
    dma = pltpu.SemaphoreType.DMA
    anywhere = pl.BlockSpec(memory_space=pl.ANY)
    return pl.pallas_call(
        functools.partial(kernel, n_tm, n_space),
        out_shape=(
            jax.ShapeDtypeStruct(base.shape, f32),
            jax.ShapeDtypeStruct(base.shape, f32),
            jax.ShapeDtypeStruct((1, COLS), f32),
        ),
        in_specs=[anywhere, anywhere],
        out_specs=(anywhere, anywhere, pl.BlockSpec(memory_space=pltpu.VMEM)),
        scratch_shapes=[
            vmem((STEPS + 1, comps, wide, ny, nz), f32),
            vmem((STEPS, 3 * comps, wide, ny, nz), f32),
            vmem((COLS, comps, wide, ny, nz), f32),
            vmem((STEPS - 1, comps, wide, ny, nz), f32),
            vmem((COLS, comps, nx, ny, nz), f32),
            vmem((comps, nx, ny, nz), f32),
            vmem((COLS, comps, nx, ny, nz), f32),
            vmem((ROWS, 8, nz), f32),
            vmem((n_space, 8, LANES), f32),
            vmem((n_tm, 8, LANES), f32),
            vmem((comps, nx, ny, nz), f32),
            vmem((comps, nx, ny, nz), f32),
            dma((2,)),
            dma((COLS + 1, 2)),
            dma((COLS + 1, 2)),
            dma((2,)),
            dma((2,)),
            dma((n_space,)),
            dma((n_space,)),
            dma((n_tm,)),
            dma((n_tm,)),
            dma((2, comps)),
        ],
        compiler_params=pltpu.CompilerParams(
            collective_id=0, has_side_effects=True, vmem_limit_bytes=44 << 20
        ),
    )(base, tangent)


def solution(mesh):
    return jax.shard_map(
        functools.partial(body, mesh.shape["tm"], mesh.shape["space"]),
        mesh=mesh,
        in_specs=(P("tm", None, "space", None, None), P("tm", None, None, "space", None, None)),
        out_specs=(
            P("tm", None, "space", None, None),
            P("tm", None, "space", None, None),
            P("tm", None),
        ),
        check_vma=False,
    )
```

profile of v0, /device:TPU:0, one launch (start us, length us, event | category | flops | bytes accessed | tf_op | source)
XLA Modules:
  0.0 88.6 jit_solution(12230437472451959774)
XLA Ops:
  0.6 0.0 copy-start
  0.6 1.4 %copy-done = f32[1,4,3,4,64,128]{5,4,3,2,1,0:T(8,128)S(1)} copy-done((f32[1,4,3,4,64,128]{5,4,3,2,1,0:T(8,128)S(1)}, f32[1,4,3,4,64,128]{5,4,3,2,1,0:T(8,128)}, u32[]{:S(2)}) %copy-start) | copy-done | bytes 1572888
  2.0 0.0 copy-start.1
  2.0 1.0 %copy-done.1 = f32[1,3,4,64,128]{4,3,2,1,0:T(8,128)S(1)} copy-done((f32[1,3,4,64,128]{4,3,2,1,0:T(8,128)S(1)}, f32[1,3,4,64,128]{4,3,2,1,0:T(8,128)}, u32[]{:S(2)}) %copy-start.1) | copy-done | bytes 393240
  3.0 83.5 %shard_map.49 = (f32[1,3,4,64,128]{4,3,2,1,0:T(8,128)S(1)}, f32[1,3,4,64,128]{4,3,2,1,0:T(8,128)S(1)}, f32[1,4]{1,0:T(1,128)S(1)}) custom-call(f32[1,3,4,64,128]{4,3,2,1,0:T(8,128)S(1)} %copy-done.1, f32[1,4,3,4,64,128]{5,4,3,2,1,0:T(8,128)S(1)} %copy-done), custom_call_target="tpu_custom_call" | custom-call | tf_op jit(solution)/shard_map/pallas_call | solution.py:348
  86.6 0.7 copy.8
  87.3 0.7 copy.9
  88.1 0.5 copy.10
Async XLA Ops:
  0.6 1.4 %copy-start = (f32[1,4,3,4,64,128]{5,4,3,2,1,0:T(8,128)S(1)}, f32[1,4,3,4,64,128]{5,4,3,2,1,0:T(8,128)}, u32[]{:S(2)}) copy-start(f32[1,4,3,4,64,128]{5,4,3,2,1,0:T(8,128)} %tangent_ref.1) | copy-start | bytes 4718596
  2.0 1.0 %copy-start.1 = (f32[1,3,4,64,128]{4,3,2,1,0:T(8,128)S(1)}, f32[1,3,4,64,128]{4,3,2,1,0:T(8,128)}, u32[]{:S(2)}) copy-start(f32[1,3,4,64,128]{4,3,2,1,0:T(8,128)} %base_ref.1) | copy-start | bytes 1179652
where the time goes:
time: 88.8 us; the launch traced here: 88.6 us
  Pallas kernels  83.5 us (94%)
  local copies, waits for them, and re-layouts  4.4 us (5%)
    pallas_call x1, Pallas kernels, body(): pl.pallas_call(functools.partial(kernel, n_tm, n_space), out_shape=(jax.S...  83.5 us
    unnamed x7, local copies, waits for them, and re-layouts  4.4 us

commit v1 on v0

--- a/solution.py
+++ b/solution.py
@@ -93,10 +93,10 @@
 
 def kernel(
     n_tm, n_space, base_ref, tangent_ref, corr_ref, defect_ref, coefs_ref,
-    flow, grads, tang, work, push, base_next, tang_next, acc, share, table,
+    flow, grads, tang, work, push, base_next, tang_next, acc, table,
     corr, defect,
     local_sem, send_sem, recv_sem, tm_send, tm_recv,
-    share_send, share_recv, table_send, table_recv, out_sem,
+    table_send, table_recv, out_sem,
 ):
     tm, space = lax.axis_index("tm"), lax.axis_index("space")
     nx = base_ref.shape[2]
@@ -106,14 +106,15 @@
     before = lax.rem(tm + n_tm - 1, n_tm)
 
     barrier = pltpu.get_barrier_semaphore()
-    for d in range(1, n_space):
-        pl.semaphore_signal(
-            barrier, inc=1, device_id={"space": lax.rem(space + d, n_space)}, device_id_type=MESH
-        )
-    for d in range(1, n_tm):
-        pl.semaphore_signal(
-            barrier, inc=1, device_id={"tm": lax.rem(tm + d, n_tm)}, device_id_type=MESH
-        )
+    order = sorted(range(n_space), key=lambda d: (d in (0,), min(d, n_space - d)))
+    others = [(d, e) for d in order for e in range(n_tm) if (d, e) != (0, 0)]
+
+    def other(offset):
+        d, e = offset
+        return {"tm": lax.rem(tm + e, n_tm), "space": lax.rem(space + d, n_space)}
+
+    for offset in others:
+        pl.semaphore_signal(barrier, inc=1, device_id=other(offset), device_id_type=MESH)
     own = pl.ds(STEPS, nx)
     local = [
         pltpu.make_async_copy(base_ref.at[0], flow.at[0, :, own], local_sem.at[0]),
@@ -121,18 +122,25 @@
     ]
     for copy in local:
         copy.start()
-    pl.semaphore_wait(barrier, n_space + n_tm - 2)
-
-    def halo(chunk, side):
-        source = pl.ds(nx - STEPS, STEPS) if side == 0 else pl.ds(0, STEPS)
-        target = pl.ds(0, STEPS) if side == 0 else pl.ds(nx + STEPS, STEPS)
+    pl.semaphore_wait(barrier, len(others))
+
+    def halo(chunk, part, side):
+        near = STEPS - 1
+        source = (
+            (pl.ds(nx - near, near), pl.ds(0, near)),
+            (pl.ds(nx - STEPS, 1), pl.ds(near, 1)),
+        )[part][side]
+        target = (
+            (pl.ds(1, near), pl.ds(nx + STEPS, near)),
+            (pl.ds(0, 1), pl.ds(wide - 1, 1)),
+        )[part][side]
         if isinstance(chunk, int) and chunk == 0:
             src, dst = base_ref.at[0, :, source], flow.at[0, :, target]
         else:
             src, dst = tangent_ref.at[0, chunk - 1, :, source], tang.at[chunk - 1, :, target]
         return pltpu.make_async_remote_copy(
             src_ref=src, dst_ref=dst,
-            send_sem=send_sem.at[chunk, side], recv_sem=recv_sem.at[chunk, side],
+            send_sem=send_sem.at[chunk, part, side], recv_sem=recv_sem.at[chunk, part, side],
             device_id={"space": up if side == 0 else down}, device_id_type=MESH,
         )
 
@@ -143,9 +151,10 @@
             device_id={"tm": before}, device_id_type=MESH,
         )
 
-    for chunk in (0, 1):
-        for side in (0, 1):
-            halo(chunk, side).start()
+    for chunk in range(COLS + 1):
+        for part in (0, 1):
+            for side in (0, 1):
+                halo(chunk, part, side).start()
     for which in (0, 1):
         tm_copy(which).start()
 
@@ -169,10 +178,9 @@
         if a != b:
             acc[b * COLS + a] = s
 
-    for side in (0, 1):
-        halo(0, side).wait()
-    for side in (0, 1):
-        halo(2, side).start()
+    for part in (0, 1):
+        for side in (0, 1):
+            halo(0, part, side).wait()
     for t in range(STEPS):
 
         def flow_step(plane, carry):
@@ -204,45 +212,52 @@
         acc[GRAM + COLS * COLS + j] = s
 
     def column(k, carry):
-        for side in (0, 1):
-            halo(k + 1, side).wait()
-
-        @pl.when(k + 3 < COLS + 1)
-        def _():
+        def tangent_step(t, plane, sums):
+            src, lead = (tang, (k,)) if t == 0 else (work, (t - 1,))
+            speed = [HALF * flow[t, d, plane] for d in range(3)]
+            own_at = [src[(*lead, d, plane)] for d in range(3)]
+            for c in range(3):
+                centre, total, *diffs = neighbours(src, (*lead, c), plane)
+                value = KEEP * centre + SPREAD * total
+                value = value - (
+                    speed[0] * diffs[0] + speed[1] * diffs[1] + speed[2] * diffs[2]
+                )
+                value = value - (
+                    own_at[0] * grads[t, 3 * c, plane]
+                    + own_at[1] * grads[t, 3 * c + 1, plane]
+                    + own_at[2] * grads[t, 3 * c + 2, plane]
+                )
+                if t < STEPS - 1:
+                    work[t, c, plane] = value
+                else:
+                    push[k, c, plane - STEPS] = value
+                    sums = tuple(
+                        s + dot_tiles(tang_next[j, c, plane - STEPS], value)
+                        for j, s in enumerate(sums)
+                    )
+            return sums
+
+        sums = (zero,) * COLS
+        for part in (0, 1):
             for side in (0, 1):
-                halo(k + 3, side).start()
-
-        for t in range(STEPS):
-
-            def tangent_step(plane, sums):
-                src, lead = (tang, (k,)) if t == 0 else (work, (t - 1,))
-                speed = [HALF * flow[t, d, plane] for d in range(3)]
-                own_at = [src[(*lead, d, plane)] for d in range(3)]
-                for c in range(3):
-                    centre, total, *diffs = neighbours(src, (*lead, c), plane)
-                    value = KEEP * centre + SPREAD * total
-                    value = value - (
-                        speed[0] * diffs[0] + speed[1] * diffs[1] + speed[2] * diffs[2]
+                halo(k + 1, part, side).wait()
+            for t in range(STEPS):
+                carried = sums if t == STEPS - 1 else ()
+                first, last = t + 1, wide - t - 2
+                if part == 0:
+                    done = lax.fori_loop(
+                        first + 1, last, functools.partial(tangent_step, t), carried
                     )
-                    value = value - (
-                        own_at[0] * grads[t, 3 * c, plane]
-                        + own_at[1] * grads[t, 3 * c + 1, plane]
-                        + own_at[2] * grads[t, 3 * c + 2, plane]
+                else:
+                    done = lax.fori_loop(
+                        0, 2,
+                        lambda i, x, t=t, first=first, last=last: tangent_step(
+                            t, first + i * (last - first), x
+                        ),
+                        carried,
                     )
-                    if t < STEPS - 1:
-                        work[t, c, plane] = value
-                    else:
-                        push[k, c, plane - STEPS] = value
-                        sums = tuple(
-                            s + dot_tiles(tang_next[j, c, plane - STEPS], value)
-                            for j, s in enumerate(sums)
-                        )
-                return sums
-
-            last = t == STEPS - 1
-            sums = lax.fori_loop(
-                t + 1, wide - t - 1, tangent_step, (zero,) * COLS if last else ()
-            )
+                if t == STEPS - 1:
+                    sums = done
         for j, s in enumerate(sums):
             acc[GRAM + k * COLS + j] = s
         return carry
@@ -253,40 +268,21 @@
     row_id = lax.broadcasted_iota(jnp.int32, (ROWS, LANES), 0)
     lane_id = lax.broadcasted_iota(jnp.int32, (ROWS, LANES), 1)
     packed = jnp.sum(jnp.where(row_id == lane_id, by_entry, 0.0), axis=0, keepdims=True)
-    share[space] = jnp.broadcast_to(packed, (8, LANES))
-
-    def share_copy(d):
+    table[space, pl.ds(tm, 1)] = packed
+
+    def table_copy(index):
+        row = table.at[space, pl.ds(tm, 1)]
         return pltpu.make_async_remote_copy(
-            src_ref=share.at[space], dst_ref=share.at[space],
-            send_sem=share_send.at[d], recv_sem=share_recv.at[d],
-            device_id={"space": lax.rem(space + d, n_space)}, device_id_type=MESH,
+            src_ref=row, dst_ref=row, send_sem=table_send.at[index], recv_sem=table_recv.at[index],
+            device_id=other(others[index]), device_id_type=MESH,
         )
 
-    def table_copy(d):
-        return pltpu.make_async_remote_copy(
-            src_ref=table.at[tm], dst_ref=table.at[tm],
-            send_sem=table_send.at[d], recv_sem=table_recv.at[d],
-            device_id={"tm": lax.rem(tm + d, n_tm)}, device_id_type=MESH,
-        )
-
-    for d in range(1, n_space):
-        share_copy(d).start()
-    for d in range(1, n_space):
-        share_copy(d).wait()
-    table[tm] = functools.reduce(jnp.add, [share[s] for s in range(n_space)])
-    for d in range(1, n_tm):
-        table_copy(d).start()
-    for d in range(1, n_tm):
-        table_copy(d).wait()
-
-    sub = lax.broadcasted_iota(jnp.int32, (8, LANES), 0)
-    groups = []
-    for g in range(max(n_tm // 8, 1)):
-        tile = jnp.zeros((8, LANES), jnp.float32)
-        for s in range(8):
-            tile = jnp.where(sub == s, table[(8 * g + s) % n_tm], tile)
-        groups.append(tile)
-    square = jnp.concatenate(groups * (LANES // (8 * len(groups))), axis=0)
+    for index in range(len(others)):
+        table_copy(index).start()
+    for index in range(len(others)):
+        table_copy(index).wait()
+    summed = functools.reduce(jnp.add, [table[d] for d in range(n_space)])
+    square = jnp.concatenate([summed] * (LANES // n_tm), axis=0)
     flipped = square.T
     coefs = shooting_coefs(lambda e: flipped[e : e + 1], n_tm)
 
@@ -363,23 +359,20 @@
             vmem((comps, nx, ny, nz), f32),
             vmem((COLS, comps, nx, ny, nz), f32),
             vmem((ROWS, 8, nz), f32),
-            vmem((n_space, 8, LANES), f32),
-            vmem((n_tm, 8, LANES), f32),
+            vmem((n_space, n_tm, LANES), f32),
             vmem((comps, nx, ny, nz), f32),
             vmem((comps, nx, ny, nz), f32),
             dma((2,)),
-            dma((COLS + 1, 2)),
-            dma((COLS + 1, 2)),
+            dma((COLS + 1, 2, 2)),
+            dma((COLS + 1, 2, 2)),
             dma((2,)),
             dma((2,)),
-            dma((n_space,)),
-            dma((n_space,)),
-            dma((n_tm,)),
-            dma((n_tm,)),
+            dma((n_space * n_tm - 1,)),
+            dma((n_space * n_tm - 1,)),
             dma((2, comps)),
         ],
         compiler_params=pltpu.CompilerParams(
-            collective_id=0, has_side_effects=True, vmem_limit_bytes=44 << 20
+            collective_id=0, has_side_effects=True, vmem_limit_bytes=59 << 20
         ),
     )(base, tangent)
 

time: 88.8 us -> 86.3 us (0.972)
  Pallas kernels: 83.5 us -> 81.4 us
    pallas_call x1, Pallas kernels: 83.5 us -> 81.4 us  [body(): pl.pallas_call(functools.partial(kernel, n_tm, n_space), out_shape=(jax.S...]
    unnamed x7 -> x5, local copies, waits for them, and re-layouts: 4.4 us -> 4.05 us
where the time goes in v1:
time: 86.3 us; the launch traced here: 86.1 us
  Pallas kernels  81.4 us (94%)
  local copies, waits for them, and re-layouts  4.05 us (5%)
    pallas_call x1, Pallas kernels, body(): pl.pallas_call(functools.partial(kernel, n_tm, n_space), out_shape=(jax.S...  81.4 us
    unnamed x5, local copies, waits for them, and re-layouts  4.05 us

profile of v1, /device:TPU:0, one launch (start us, length us, event | category | flops | bytes accessed | tf_op | source)
XLA Modules:
  0.0 86.1 jit_solution(10231702960633647986)
XLA Ops:
  0.6 81.4 %shard_map.49 = (f32[1,3,4,64,128]{4,3,2,1,0:T(8,128)}, f32[1,3,4,64,128]{4,3,2,1,0:T(8,128)}, f32[1,4]{1,0:T(1,128)}) custom-call(f32[1,3,4,64,128]{4,3,2,1,0:T(8,128)} %base_ref.1, f32[1,4,3,4,64,128]{5,4,3,2,1,0:T(8,128)} %tangent_ref.1), custom_call_target="tpu_custom_call" | custom-call | tf_op jit(solution)/shard_map/pallas_call | solution.py:344
  82.1 0.0 copy-start
  82.1 1.8 %copy.8 = f32[1,3,4,64,128]{4,3,2,1,0:T(8,128)} copy(f32[1,3,4,64,128]{4,3,2,1,0:T(8,128)} %get-tuple-element.6) | data formatting | bytes 786432
  83.8 1.8 %copy.9 = f32[1,3,4,64,128]{4,3,2,1,0:T(8,128)} copy(f32[1,3,4,64,128]{4,3,2,1,0:T(8,128)} %get-tuple-element.7) | data formatting | bytes 786432
  85.6 0.0 copy-done
  85.6 0.5 copy.10
Async XLA Ops:
  82.1 3.5 %copy-start = (f32[1,4]{1,0:T(1,128)S(1)}, f32[1,4]{1,0:T(1,128)}, u32[]{:S(2)}) copy-start(f32[1,4]{1,0:T(1,128)} %get-tuple-element.8) | copy-start | bytes 52

commit v2 on v1

--- a/solution.py
+++ b/solution.py
@@ -92,11 +92,10 @@
 
 
 def kernel(
-    n_tm, n_space, base_ref, tangent_ref, corr_ref, defect_ref, coefs_ref,
+    n_tm, n_space, base_ref, tangent_ref, push_out, gap_out, next_out, values_ref,
     flow, grads, tang, work, push, base_next, tang_next, acc, table,
-    corr, defect,
     local_sem, send_sem, recv_sem, tm_send, tm_recv,
-    table_send, table_recv, out_sem,
+    table_send, table_recv, near, out_sem,
 ):
     tm, space = lax.axis_index("tm"), lax.axis_index("space")
     nx = base_ref.shape[2]
@@ -113,8 +112,9 @@
         d, e = offset
         return {"tm": lax.rem(tm + e, n_tm), "space": lax.rem(space + d, n_space)}
 
-    for offset in others:
-        pl.semaphore_signal(barrier, inc=1, device_id=other(offset), device_id_type=MESH)
+    beside = ({"space": up}, {"space": down}, {"tm": lax.rem(tm + 1, n_tm)}, {"tm": before})
+    for device in beside:
+        pl.semaphore_signal(barrier, inc=1, device_id=device, device_id_type=MESH)
     own = pl.ds(STEPS, nx)
     local = [
         pltpu.make_async_copy(base_ref.at[0], flow.at[0, :, own], local_sem.at[0]),
@@ -122,7 +122,7 @@
     ]
     for copy in local:
         copy.start()
-    pl.semaphore_wait(barrier, len(others))
+    pl.semaphore_wait(barrier, len(beside))
 
     def halo(chunk, part, side):
         near = STEPS - 1
@@ -158,6 +158,15 @@
     for which in (0, 1):
         tm_copy(which).start()
 
+    def pass_on(i, carry):
+        for side, device in enumerate(beside):
+            pl.semaphore_signal(near.at[side ^ 1], inc=1, device_id=device, device_id_type=MESH)
+        for side in range(len(beside)):
+            pl.semaphore_wait(near.at[side], 1)
+        return carry
+
+    lax.fori_loop(0, n_space // 2 + n_tm // 2 - 1, pass_on, 0)
+
     height = lax.broadcasted_iota(jnp.int32, (ny, nz), 0).astype(jnp.float32)
     drive = (time_step * forcing_amp) * jnp.sin(2.0 * jnp.pi * wave_number * height / ny)
 
@@ -210,6 +219,14 @@
     sums = lax.fori_loop(0, 3 * nx, end_step, (zero,) * COLS)
     for j, s in enumerate(sums):
         acc[GRAM + COLS * COLS + j] = s
+
+    gap_copy = pltpu.make_async_copy(base_next, gap_out, out_sem.at[COLS])
+    next_copy = pltpu.make_async_copy(tang_next, next_out, out_sem.at[COLS + 1])
+    gap_copy.start()
+    next_copy.start()
+
+    def push_copy(k):
+        return pltpu.make_async_copy(push.at[k], push_out.at[k], out_sem.at[k])
 
     def column(k, carry):
         def tangent_step(t, plane, sums):
@@ -260,6 +277,7 @@
                     sums = done
         for j, s in enumerate(sums):
             acc[GRAM + k * COLS + j] = s
+        push_copy(k).start()
         return carry
 
     lax.fori_loop(0, COLS, column, 0)
@@ -294,44 +312,38 @@
         axis=0,
     )
     values = jnp.sum(both, axis=1, keepdims=True)
-    own_c = [values[k : k + 1] for k in range(COLS)]
-    next_c = [values[COLS + k : COLS + k + 1] for k in range(COLS)]
+    values_ref[...] = jnp.broadcast_to(values, (2 * COLS, LANES))
+    for k in range(COLS):
+        push_copy(k).wait()
+    gap_copy.wait()
+    next_copy.wait()
+
+
+def finish_kernel(tang, push, gap, tang_next, values, corr, defect, coefs):
+    nx, ny, nz = gap.shape[1:]
     places = lax.broadcasted_iota(jnp.int32, (1, COLS), 1)
     out = jnp.zeros((1, COLS), jnp.float32)
     for k in range(COLS):
-        out = jnp.where(places == k, own_c[k], out)
-    coefs_ref[...] = out
-
-    def out_copy(which, comp):
-        src, dst = ((corr, corr_ref), (defect, defect_ref))[which]
-        return pltpu.make_async_copy(src.at[comp], dst.at[0, comp], out_sem.at[which, comp])
-
-    own_b = [jnp.broadcast_to(x, (8, LANES)) for x in own_c]
-    next_b = [jnp.broadcast_to(x, (8, LANES)) for x in next_c]
+        out = jnp.where(places == k, values[k : k + 1, :COLS], out)
+    coefs[...] = out
+    own = [jnp.broadcast_to(values[k : k + 1], (8, LANES)) for k in range(COLS)]
+    following = [jnp.broadcast_to(values[COLS + k : COLS + k + 1], (8, LANES)) for k in range(COLS)]
 
     def scaled(coef, array):
         return (array.reshape(ny // 8, 8, nz) * coef[None]).reshape(ny, nz)
 
-    for comp in range(3):
-
-        def finish(plane, carry):
-            terms = [scaled(own_b[k], tang[k, comp, plane + STEPS]) for k in range(COLS)]
-            corr[comp, plane] = (terms[0] + terms[1]) + (terms[2] + terms[3])
-            value = base_next[comp, plane]
-            for k in range(COLS):
-                value = value + (
-                    scaled(own_b[k], push[k, comp, plane])
-                    - scaled(next_b[k], tang_next[k, comp, plane])
-                )
-            defect[comp, plane] = value
-            return carry
-
-        lax.fori_loop(0, nx, finish, 0)
-        out_copy(0, comp).start()
-        out_copy(1, comp).start()
-    for comp in range(3):
-        out_copy(0, comp).wait()
-        out_copy(1, comp).wait()
+    def finish(plane, carry):
+        terms = [scaled(own[k], tang[0, k, 0, plane]) for k in range(COLS)]
+        corr[0, 0, plane] = (terms[0] + terms[1]) + (terms[2] + terms[3])
+        value = gap[0, plane]
+        for k in range(COLS):
+            value = value + (
+                scaled(own[k], push[k, 0, plane]) - scaled(following[k], tang_next[k, 0, plane])
+            )
+        defect[0, 0, plane] = value
+        return carry
+
+    lax.fori_loop(0, nx, finish, 0)
 
 
 def body(n_tm, n_space, base, tangent):
@@ -341,15 +353,16 @@
     vmem = pltpu.VMEM
     dma = pltpu.SemaphoreType.DMA
     anywhere = pl.BlockSpec(memory_space=pl.ANY)
-    return pl.pallas_call(
+    push, gap, tang_next, values = pl.pallas_call(
         functools.partial(kernel, n_tm, n_space),
         out_shape=(
-            jax.ShapeDtypeStruct(base.shape, f32),
-            jax.ShapeDtypeStruct(base.shape, f32),
-            jax.ShapeDtypeStruct((1, COLS), f32),
+            jax.ShapeDtypeStruct((COLS, comps, nx, ny, nz), f32),
+            jax.ShapeDtypeStruct((comps, nx, ny, nz), f32),
+            jax.ShapeDtypeStruct((COLS, comps, nx, ny, nz), f32),
+            jax.ShapeDtypeStruct((2 * COLS, LANES), f32),
         ),
         in_specs=[anywhere, anywhere],
-        out_specs=(anywhere, anywhere, pl.BlockSpec(memory_space=pltpu.VMEM)),
+        out_specs=(anywhere, anywhere, anywhere, pl.BlockSpec(memory_space=pltpu.VMEM)),
         scratch_shapes=[
             vmem((STEPS + 1, comps, wide, ny, nz), f32),
             vmem((STEPS, 3 * comps, wide, ny, nz), f32),
@@ -360,8 +373,6 @@
             vmem((COLS, comps, nx, ny, nz), f32),
             vmem((ROWS, 8, nz), f32),
             vmem((n_space, n_tm, LANES), f32),
-            vmem((comps, nx, ny, nz), f32),
-            vmem((comps, nx, ny, nz), f32),
             dma((2,)),
             dma((COLS + 1, 2, 2)),
             dma((COLS + 1, 2, 2)),
@@ -369,12 +380,34 @@
             dma((2,)),
             dma((n_space * n_tm - 1,)),
             dma((n_space * n_tm - 1,)),
-            dma((2, comps)),
+            pltpu.SemaphoreType.REGULAR((4,)),
+            dma((COLS + 2,)),
         ],
         compiler_params=pltpu.CompilerParams(
-            collective_id=0, has_side_effects=True, vmem_limit_bytes=59 << 20
+            collective_id=0, has_side_effects=True, vmem_limit_bytes=44 << 20
         ),
-    )(base, tangent)
+    )(pltpu.with_memory_space_constraint(base, pltpu.HBM), pltpu.with_memory_space_constraint(tangent, pltpu.HBM))
+    block = (nx, ny, nz)
+    columns = pl.BlockSpec((COLS, 1, *block), lambda c: (0, c, 0, 0, 0))
+    field = pl.BlockSpec((1, 1, *block), lambda c: (0, c, 0, 0, 0))
+    return pl.pallas_call(
+        finish_kernel,
+        grid=(comps,),
+        out_shape=(
+            jax.ShapeDtypeStruct(base.shape, f32),
+            jax.ShapeDtypeStruct(base.shape, f32),
+            jax.ShapeDtypeStruct((1, COLS), f32),
+        ),
+        in_specs=[
+            pl.BlockSpec((1, COLS, 1, *block), lambda c: (0, 0, c, 0, 0, 0)),
+            columns,
+            pl.BlockSpec((1, *block), lambda c: (c, 0, 0, 0)),
+            columns,
+            pl.BlockSpec((2 * COLS, LANES), lambda c: (0, 0)),
+        ],
+        out_specs=(field, field, pl.BlockSpec((1, COLS), lambda c: (0, 0))),
+        compiler_params=pltpu.CompilerParams(vmem_limit_bytes=24 << 20),
+    )(tangent, push, gap, tang_next, values)
 
 
 def solution(mesh):

time: 86.3 us -> 81.9 us (0.949)
  local copies, waits for them, and re-layouts: 4.05 us -> 0.01 us
    unnamed x5 -> x2, local copies, waits for them, and re-layouts: 4.05 us -> 0.01 us
    pallas_call x1, Pallas kernels: 81.4 us -> 79.2 us  [body(): pl.pallas_call(functools.partial(kernel, n_tm, n_space), out_shape=(jax.S...]
    pallas_call x0 -> x1, Pallas kernels: none -> 1.91 us  [body(): pl.pallas_call(finish_kernel, grid=(comps,), out_shape=(jax.ShapeDtypeStr...]
where the time goes in v2:
time: 81.9 us; the launch traced here: 81.7 us
  Pallas kernels  81.1 us (99%)
    pallas_call x1, Pallas kernels, body(): pl.pallas_call(functools.partial(kernel, n_tm, n_space), out_shape=(jax.S...  79.2 us
    pallas_call x1, Pallas kernels, body(): pl.pallas_call(finish_kernel, grid=(comps,), out_shape=(jax.ShapeDtypeStr...  1.91 us

profile of v2, /device:TPU:0, one launch (start us, length us, event | category | flops | bytes accessed | tf_op | source)
XLA Modules:
  0.0 81.7 jit_solution(2215197092709909921)
XLA Ops:
  0.6 0.0 copy-start
  0.6 79.2 %shard_map.49 = (f32[4,3,4,64,128]{4,3,2,1,0:T(8,128)S(1)}, f32[3,4,64,128]{3,2,1,0:T(8,128)S(1)}, f32[4,3,4,64,128]{4,3,2,1,0:T(8,128)S(1)}, f32[8,128]{1,0:T(8,128)S(1)}) custom-call(f32[1,3,4,64,128]{4,3,2,1,0:T(8,128)} %base_ref.1, f32[1,4,3,4,64,128]{5,4,3,2,1,0:T(8,128)} %tang.1), custom_call_target="tpu_custom_call" | custom-call | tf_op jit(solution)/shard_map/pallas_call | solution.py:356
  79.8 0.0 copy-done
  79.8 1.9 %shard_map.50 = (f32[1,3,4,64,128]{4,3,2,1,0:T(8,128)}, f32[1,3,4,64,128]{4,3,2,1,0:T(8,128)}, f32[1,4]{1,0:T(1,128)}) custom-call(f32[1,4,3,4,64,128]{5,4,3,2,1,0:T(8,128)S(1)} %copy-done, f32[4,3,4,64,128]{4,3,2,1,0:T(8,128)S(1)} %get-tuple-element.7.push, f32[3,4,64,128]{3,2,1,0:T(8,128)S(1)} %get-tuple-element.8.gap, ...), custom_call_target="tpu_custom_call" | custom-call | tf_op jit(solution)/shard_map/pallas_call | solution.py:393
Async XLA Ops:
  0.6 79.2 %copy-start = (f32[1,4,3,4,64,128]{5,4,3,2,1,0:T(8,128)S(1)}, f32[1,4,3,4,64,128]{5,4,3,2,1,0:T(8,128)}, u32[]{:S(2)}) copy-start(f32[1,4,3,4,64,128]{5,4,3,2,1,0:T(8,128)} %tang.1) | copy-start | bytes 4718596
